TPU v7x, 32 devices: a whole 2x2x4 slice. The times are simulated.
32 devices in a mesh: seq: 4 (over z), pair: 4 (over y, core), dp: 2 (over x).
Axes of the slice: x: 2, y: 2, z: 4, core: 2. Of those that a mesh axis runs over, the one named last changes fastest.
Arguments:
- embed: bfloat16 [2048, 1536], P(('dp', 'seq')), parts along dimension 0, may hold values from -6 to 6
- attn_gain: float32 [1536], replicated, may hold values from 0.5 to 1.5
- w_query: bfloat16 [1536, 1024], P(None, 'pair'), may hold values from -2.5643096 to 2.5643096
- w_key: bfloat16 [1536, 128], replicated, may hold values from -0.104613624 to 0.104613624
- w_value: bfloat16 [1536, 128], replicated, may hold values from -0.15625 to 0.15625
- w_out: bfloat16 [1024, 1536], P('pair'), may hold values from -0.1875 to 0.1875
- pair_map: bfloat16 [128, 64, 128], P(('dp', 'seq'), 'pair'), parts along dimension 0, may hold values from -6 to 6
- w_row: bfloat16 [1536, 128], replicated, may hold values from -0.625 to 0.625
- w_col: bfloat16 [1536, 128], replicated, may hold values from -0.625 to 0.625
- pair_gain: float32 [128], replicated, may hold values from 0.5 to 1.5
- conv_weight: bfloat16 [3, 3, 128, 128], replicated, may hold values from -0.1875 to 0.1875
Outputs:
- block_out: bfloat16 [2048, 1536], P(('dp', 'seq'), 'pair'), parts along dimension 0
- new_pair: bfloat16 [128, 64, 128], P(('dp', 'seq'), 'pair'), parts along dimension 0
There are 2 independent parts, one for each index of `dp`. A program takes and returns all parts, laid end to end along the dimension named above; an argument that names none is the same for every part. Nothing has to cross between parts.
All inputs are finite; a program needn't handle non-finite values.
Results may differ from a plain program's by a relative error of at most 0.014.
Values may be sent and summed in bfloat16 or wider, within the bound.
A program may use at most 64 MiB of HBM per device.

v0:
```python
import math

import jax
import jax.numpy as jnp
from jax import lax
from jax.sharding import PartitionSpec as P

POOL = 16


def padded_2(block, sides, width):
    for axis, dim in sides:
        count = lax.axis_size(axis)
        forward = [(i, i + 1) for i in range(count - 1)]
        backward = [(target, source) for source, target in forward]
        low = lax.ppermute(
            lax.slice_in_dim(block, block.shape[dim] - width, None, axis=dim), axis, forward
        )
        high = lax.ppermute(lax.slice_in_dim(block, 0, width, axis=dim), axis, backward)
        block = jnp.concatenate([low, block, high], axis=dim)
    return block


def rms_scale(values, gain):
    return values * lax.rsqrt(jnp.mean(values * values, axis=-1, keepdims=True) + 1e-05) * gain


def rotate(tensor, positions):
    half = tensor.shape[-1] // 2
    freq = 10000.0 ** (-jnp.arange(half, dtype=jnp.float32) / half)
    angles = positions[:, None] * freq[None, :]
    cosine = jnp.cos(angles)[:, None, :]
    sine = jnp.sin(angles)[:, None, :]
    first = tensor[..., :half]
    second = tensor[..., half:]
    return jnp.concatenate(
        [first * cosine - second * sine, first * sine + second * cosine], axis=-1
    )


def per_device(
    embed, attn_gain, w_query, w_key, w_value, w_out, pair_map, w_row, w_col, pair_gain, conv_weight
):
    tokens = embed.shape[0]
    head_size = w_key.shape[1]
    local_heads = w_query.shape[1] // head_size
    normed = rms_scale(embed.astype(jnp.float32), attn_gain).astype(jnp.bfloat16)
    positions = (lax.axis_index("seq") * tokens + jnp.arange(tokens)).astype(jnp.float32)
    query = jnp.dot(normed, w_query, preferred_element_type=jnp.float32).reshape(
        tokens, local_heads, head_size
    )
    query = rotate(query, positions).transpose(1, 0, 2).astype(jnp.bfloat16)
    key = jnp.dot(normed, w_key, preferred_element_type=jnp.float32)[:, None, :]
    key = rotate(key, positions)[:, 0, :].astype(jnp.bfloat16)
    value = jnp.dot(normed, w_value, preferred_element_type=jnp.float32).astype(jnp.bfloat16)
    scale = 1.0 / head_size**0.5

    def attend_block(carry, block):
        running_max, running_sum, running_acc = carry
        key_block, value_block = block
        scores = (
            jnp.einsum("hqd,kd->hqk", query, key_block, preferred_element_type=jnp.float32) * scale
        )
        new_max = jnp.maximum(running_max, jnp.max(scores, axis=-1))
        factor = jnp.exp(running_max - new_max)
        terms = jnp.exp(scores - new_max[..., None])
        new_sum = running_sum * factor + jnp.sum(terms, axis=-1)
        mixed = jnp.einsum(
            "hqk,kd->hqd",
            terms.astype(jnp.bfloat16),
            value_block,
            preferred_element_type=jnp.float32,
        )
        return ((new_max, new_sum, running_acc * factor[..., None] + mixed), None)

    initial = (
        jnp.full((local_heads, tokens), -1e30, jnp.float32),
        jnp.zeros((local_heads, tokens), jnp.float32),
        jnp.zeros((local_heads, tokens, head_size), jnp.float32),
    )
    key_piece = lax.all_gather(key, "seq", axis=0, tiled=True)
    value_piece = lax.all_gather(value, "seq", axis=0, tiled=True)
    length = key_piece.shape[0]
    block = math.gcd(length, 1024)
    key_blocks = key_piece.reshape(length // block, block, head_size)
    value_blocks = value_piece.reshape(length // block, block, head_size)
    result, unused = lax.scan(attend_block, initial, (key_blocks, value_blocks))
    final_max, final_sum, final_acc = result
    attended = (final_acc / final_sum[..., None]).astype(jnp.bfloat16)
    attended = attended.transpose(1, 0, 2).reshape(tokens, local_heads * head_size)
    head_terms = jnp.dot(attended, w_out, preferred_element_type=jnp.float32)
    summed = lax.psum_scatter(
        head_terms.astype(jnp.bfloat16), "pair", scatter_dimension=1, tiled=True
    ).astype(jnp.float32)
    feature_count = summed.shape[1]
    residual = lax.dynamic_slice_in_dim(
        embed, lax.axis_index("pair") * feature_count, feature_count, 1
    )
    block_out = (residual.astype(jnp.float32) + summed).astype(jnp.bfloat16)
    model_width = normed.shape[1]
    pooled = jnp.mean(
        normed.astype(jnp.float32).reshape(tokens // POOL, POOL, model_width), axis=1
    ).astype(jnp.bfloat16)
    row_feat = jnp.dot(pooled, w_row, preferred_element_type=jnp.float32).astype(jnp.bfloat16)
    col_feat = jnp.dot(pooled, w_col, preferred_element_type=jnp.float32).astype(jnp.bfloat16)
    all_cols = lax.all_gather(col_feat, "seq", axis=0, tiled=True)
    column_count = pair_map.shape[1]
    my_cols = lax.dynamic_slice_in_dim(
        all_cols, lax.axis_index("pair") * column_count, column_count, 0
    )
    updated = (
        pair_map.astype(jnp.float32)
        + row_feat.astype(jnp.float32)[:, None, :] * my_cols.astype(jnp.float32)[None, :, :]
    )
    pair_normed = rms_scale(updated, pair_gain).astype(jnp.bfloat16)
    padded = padded_2(pair_normed, (("seq", 0), ("pair", 1)), 1)
    row_count = pair_map.shape[0]
    channel_count = pair_map.shape[2]
    convolved = jnp.zeros((row_count * column_count, channel_count), jnp.float32)
    for offset_row in range(3):
        for offset_col in range(3):
            window = padded[
                offset_row : offset_row + row_count, offset_col : offset_col + column_count, :
            ]
            convolved = convolved + jnp.dot(
                window.reshape(row_count * column_count, channel_count),
                conv_weight[offset_row, offset_col],
                preferred_element_type=jnp.float32,
            )
    new_pair = (updated + convolved.reshape(row_count, column_count, channel_count)).astype(
        jnp.bfloat16
    )
    return (block_out, new_pair)


def solution(mesh):
    placed = (
        P(("dp", "seq"), None),
        P(),
        P(None, "pair"),
        P(),
        P(),
        P("pair", None),
        P(("dp", "seq"), "pair", None),
        P(),
        P(),
        P(),
        P(),
    )
    return jax.shard_map(
        per_device,
        mesh=mesh,
        in_specs=placed,
        out_specs=(P(("dp", "seq"), "pair"), P(("dp", "seq"), "pair", None)),
        check_vma=False,
    )
```

profile of v0, /device:TPU:1, one launch (start us, length us, event | category | flops | bytes accessed | tf_op | source)
XLA Modules:
  0.0 97.0 jit_solution(4122709407723177928)
XLA Ops:
  7.2 0.0 copy-start
  7.2 0.0 copy-start.1
  7.2 0.0 copy-start.6
  7.2 0.0 copy-start.4
  7.2 0.0 copy-start.3
  7.2 0.0 copy-start.2
  7.2 0.0 copy-start.7
  7.2 0.0 copy-start.9
  7.3 0.0 reduce-scatter.4.cloned.1.call-start
  7.3 1.5 %fusion.2 = f32[256]{0:T(256)S(1)} fusion(bf16[256,1536]{1,0:T(8,128)(2,1)} %param.11), kind=kLoop, calls=%fused_computation.7 | loop fusion | flops 1179392 | bytes 787456 | tf_op jit(solution)/shard_map/reduce_sum | solution.py:25
  8.8 1.7 %convert_reduce_fusion = f32[16,1536]{1,0:T(8,128)S(1)} fusion(f32[1536]{0:T(1024)} %param.12, f32[256]{0:T(256)S(1)} %add_rsqrt_fusion.1, bf16[256,1536]{1,0:T(8,128)(2,1)} %param.11), kind=kLoop, calls=%fused_computation.10 | loop fusion | flops 2334720 | bytes 891904 | tf_op jit(solution)/shard_map/reduce_sum | solution.py:101
  10.5 0.0 copy-done.4
  10.5 0.2 convolution_convert_fusion.2
  10.7 11.3 %all_gather.11 = bf16[64,128]{1,0:T(8,128)(2,1)S(1)} all-gather(bf16[16,128]{1,0:T(8,128)(2,1)S(1)} %convolution_convert_fusion.2), channel_id=1, replica_groups=mesh['seq'=4,'pair'=4,'dp'=2] {'seq'}, dimensions={0}, use_global_device_ids=true | all-gather | bytes 20480 | tf_op jit(solution)/shard_map/all_gather | solution.py:106
  22.0 0.0 copy-done.3
  22.0 0.2 fusion.9
  22.2 0.0 copy-done.2
  22.2 0.1 multiply_reduce_fusion.1
  22.3 0.0 copy-done.7
  22.3 0.1 multiply_convert_fusion
  22.4 1.3 %collective-permute-start.1 = (bf16[1,16,128]{2,1,0:T(8,128)(2,1)S(1)}, bf16[1,16,128]{2,1,0:T(8,128)(2,1)S(1)}, u32[]{:S(2)}, u32[]{:S(2)}) collective-permute-start(bf16[1,16,128]{2,1,0:T(8,128)(2,1)S(1)} %get-tuple-element.42), channel_id=1, source_target_pairs={{8,0},{16,8},{24,16},{9,1},{17,9},{25,17},{10,2},{18,10},{26,18},{... | collective-permute-start | bytes 12296 | tf_op jit(solution)/shard_map/ppermute | solution.py:19
  23.7 4.0 %collective-permute-start = (bf16[1,16,128]{2,1,0:T(8,128)(2,1)S(1)}, bf16[1,16,128]{2,1,0:T(8,128)(2,1)S(1)}, u32[]{:S(2)}, u32[]{:S(2)}) collective-permute-start(bf16[1,16,128]{2,1,0:T(8,128)(2,1)S(1)} %get-tuple-element.41), channel_id=1, source_target_pairs={{0,8},{8,16},{16,24},{1,9},{9,17},{17,25},{2,10},{10,18},{18,26},{... | collective-permute-start | bytes 12296 | tf_op jit(solution)/shard_map/ppermute | solution.py:16
  27.8 0.5 convolution_bitcast_fusion.1
  28.3 0.5 multiply_cosine_fusion
  28.8 0.3 fusion.23
  29.1 11.1 %all-gather = bf16[1024,1,128]{0,2,1:T(8,128)(2,1)S(1)} all-gather(bf16[256,1,128]{0,2,1:T(8,128)(2,1)S(1)} %pad_maximum_fusion.3), channel_id=2, replica_groups=mesh['seq'=4,'pair'=4,'dp'=2] {'seq'}, dimensions={0}, use_global_device_ids=true | all-gather | bytes 327680 | tf_op jit(solution)/shard_map/all_gather | solution.py:81
  40.3 0.0 copy-done.8
  40.3 0.6 fusion.52
  40.9 0.1 copy.24
  41.0 0.1 copy.23
  41.1 0.1 subtract_convert_fusion
  41.2 0.0 copy-start.10
  41.2 0.6 multiply_reduce_fusion
  41.8 0.4 copy-done.10
  42.2 0.5 convolution_convert_fusion.1
  42.7 11.0 %all_gather.10 = bf16[1024,128]{0,1:T(8,128)(2,1)S(1)} all-gather(bf16[256,128]{0,1:T(8,128)(2,1)S(1)} %convolution_convert_fusion.1), channel_id=1, replica_groups=mesh['seq'=4,'pair'=4,'dp'=2] {'seq'}, dimensions={0}, use_global_device_ids=true | all-gather | bytes 327680 | tf_op jit(solution)/shard_map/all_gather | solution.py:82
  53.7 0.5 fusion
  54.2 0.6 fusion.7
  54.8 0.0 copy-done
  54.8 0.4 convolution_convert_fusion
  55.2 0.0 copy-start.5
  55.2 1.2 %copy.21 = bf16[256,1536]{0,1:T(8,128)(2,1)} copy(bf16[256,1536]{1,0:T(8,128)(2,1)S(1)} %convolution_convert_fusion) | data formatting | bytes 1572864
  56.4 0.0 reduce-scatter.4.cloned.1.call-update
  56.4 0.0 collective-permute-done.1
  56.4 0.0 collective-permute-done
  56.5 12.7 %collective-permute-start.2 = (bf16[18,1,128]{2,1,0:T(2,128)(2,1)S(1)}, bf16[18,1,128]{2,1,0:T(2,128)(2,1)S(1)}, u32[]{:S(2)}, u32[]{:S(2)}) collective-permute-start(bf16[18,1,128]{2,1,0:T(2,128)(2,1)S(1)} %get-tuple-element.37), channel_id=1, source_target_pairs={{0,2},{2,4},{4,6},{1,3},{3,5},{5,7},{8,10},{10,12},{12,14},{9,11},... | collective-permute-start | bytes 13832 | tf_op jit(solution)/shard_map/ppermute | solution.py:16
  69.2 1.9 %collective-permute-start.3 = (bf16[18,1,128]{2,1,0:T(2,128)(2,1)S(1)}, bf16[18,1,128]{2,1,0:T(2,128)(2,1)S(1)}, u32[]{:S(2)}, u32[]{:S(2)}) collective-permute-start(bf16[18,1,128]{2,1,0:T(2,128)(2,1)S(1)} %get-tuple-element.38), channel_id=1, source_target_pairs={{2,0},{4,2},{6,4},{3,1},{5,3},{7,5},{10,8},{12,10},{14,12},{11,9},... | collective-permute-start | bytes 13832 | tf_op jit(solution)/shard_map/ppermute | solution.py:19
  71.1 0.1 fusion.34
  71.3 0.0 collective-permute-done.2
  71.3 2.9 %collective-permute-done.3 = bf16[18,1,128]{2,1,0:T(2,128)(2,1)S(1)} collective-permute-done((bf16[18,1,128]{2,1,0:T(2,128)(2,1)S(1)}, bf16[18,1,128]{2,1,0:T(2,128)(2,1)S(1)}, u32[]{:S(2)}, u32[]{:S(2)}) %collective-permute-start.3) | collective-permute-done | bytes 4640 | tf_op jit(solution)/shard_map/ppermute | solution.py:19
  74.1 0.1 maximum_maximum_fusion
  74.2 0.1 fusion.55
  74.3 0.1 convolution_add_fusion.6
  74.4 0.1 convolution_add_fusion.5
  74.6 0.1 fusion.26
  74.7 0.2 convolution_add_fusion.4
  74.9 0.1 convolution_add_fusion.3
  75.0 0.1 convolution_add_fusion.2
  75.2 0.1 convolution_add_fusion.1
  75.3 0.1 fusion.8
  75.5 0.7 add_convert_fusion.2
  76.1 12.2 %reduce-scatter.4.cloned.1.call-done = bf16[384,256]{1,0:T(8,128)(2,1)} async-done(((bf16[1536,256]{1,0:T(8,128)(2,1)}), bf16[384,256]{1,0:T(8,128)(2,1)}) %reduce-scatter.4.cloned.1.call-update) | async-done | bytes 196624
  88.3 1.1 %copy.22 = bf16[256,384]{1,0:T(8,128)(2,1)S(1)} copy(bf16[256,384]{0,1:T(8,128)(2,1)} %bitcast.103) | data formatting | bytes 393216
  89.4 0.7 add_convert_fusion
  (17 shorter events, 0.1 us)
Async XLA Ops:
  7.2 47.7 %copy-start = (bf16[256,1536]{1,0:T(8,128)(2,1)S(1)}, bf16[256,1536]{1,0:T(8,128)(2,1)}, u32[]{:S(2)}) copy-start(bf16[256,1536]{1,0:T(8,128)(2,1)} %param.16) | copy-start | bytes 2359300
  7.2 20.6 %copy-start.1 = (bf16[256,1536]{1,0:T(8,128)(2,1)S(1)}, bf16[256,1536]{1,0:T(8,128)(2,1)}, u32[]{:S(2)}) copy-start(bf16[256,1536]{1,0:T(8,128)(2,1)} %param.11) | copy-start | bytes 2359300
  7.2 20.5 %copy-start.6 = (f32[1536]{0:T(1024)S(1)}, f32[1536]{0:T(1024)}, u32[]{:S(2)}) copy-start(f32[1536]{0:T(1024)} %param.12) | copy-start | bytes 18436
  7.2 3.3 %copy-start.4 = (bf16[1536,128]{1,0:T(8,128)(2,1)S(1)}, bf16[1536,128]{1,0:T(8,128)(2,1)}, u32[]{:S(2)}) copy-start(bf16[1536,128]{1,0:T(8,128)(2,1)} %param.19) | copy-start | bytes 1179652
  7.2 14.8 %copy-start.3 = (bf16[1536,128]{1,0:T(8,128)(2,1)S(1)}, bf16[1536,128]{1,0:T(8,128)(2,1)}, u32[]{:S(2)}) copy-start(bf16[1536,128]{1,0:T(8,128)(2,1)} %param.18) | copy-start | bytes 1179652
  7.2 14.9 %copy-start.2 = (bf16[16,16,128]{2,1,0:T(8,128)(2,1)S(1)}, bf16[16,16,128]{2,1,0:T(8,128)(2,1)}, u32[]{:S(2)}) copy-start(bf16[16,16,128]{2,1,0:T(8,128)(2,1)} %param.17) | copy-start | bytes 196612
  7.2 15.1 %copy-start.7 = (f32[128]{0:T(128)S(1)}, f32[128]{0:T(128)}, u32[]{:S(2)}) copy-start(f32[128]{0:T(128)} %param.20) | copy-start | bytes 1540
  7.2 20.5 %copy-start.9 = (bf16[1536,128]{1,0:T(8,128)(2,1)S(1)}, bf16[1536,128]{1,0:T(8,128)(2,1)}, u32[]{:S(2)}) copy-start(bf16[1536,128]{1,0:T(8,128)(2,1)} %param.14) | copy-start | bytes 1179652
  7.3 81.0 %reduce-scatter.4.cloned.1.call-start = ((), (), s32[]{:S(2)}) async-start(), calls=%async_computation.1 | async-start | bytes 983040
  22.0 18.3 %copy-start.8 = (bf16[1536,256]{1,0:T(8,128)(2,1)S(1)}, bf16[1536,256]{1,0:T(8,128)(2,1)}, u32[]{:S(2)}) copy-start(bf16[1536,256]{1,0:T(8,128)(2,1)} %param.13) | copy-start | bytes 2359300
  22.4 34.0 %collective-permute-start.1 = (bf16[1,16,128]{2,1,0:T(8,128)(2,1)S(1)}, bf16[1,16,128]{2,1,0:T(8,128)(2,1)S(1)}, u32[]{:S(2)}, u32[]{:S(2)}) collective-permute-start(bf16[1,16,128]{2,1,0:T(8,128)(2,1)S(1)} %get-tuple-element.42), channel_id=1, source_target_pairs={{8,0},{16,8},{24,16},{9,1},{17,9},{25,17},{10,2},{18,10},{26,18},{... | collective-permute-start | bytes 12296 | tf_op jit(solution)/shard_map/ppermute | solution.py:19
  23.7 32.7 %collective-permute-start = (bf16[1,16,128]{2,1,0:T(8,128)(2,1)S(1)}, bf16[1,16,128]{2,1,0:T(8,128)(2,1)S(1)}, u32[]{:S(2)}, u32[]{:S(2)}) collective-permute-start(bf16[1,16,128]{2,1,0:T(8,128)(2,1)S(1)} %get-tuple-element.41), channel_id=1, source_target_pairs={{0,8},{8,16},{16,24},{1,9},{9,17},{17,25},{2,10},{10,18},{18,26},{... | collective-permute-start | bytes 12296 | tf_op jit(solution)/shard_map/ppermute | solution.py:16
  41.2 1.0 %copy-start.10 = (bf16[1536,128]{1,0:T(8,128)(2,1)S(1)}, bf16[1536,128]{1,0:T(8,128)(2,1)}, u32[]{:S(2)}) copy-start(bf16[1536,128]{1,0:T(8,128)(2,1)} %param.15) | copy-start | bytes 1179652
  55.2 15.9 %copy-start.5 = (bf16[3,3,128,128]{3,2,1,0:T(8,128)(2,1)S(1)}, bf16[3,3,128,128]{3,2,1,0:T(8,128)(2,1)}, u32[]{:S(2)}) copy-start(bf16[3,3,128,128]{3,2,1,0:T(8,128)(2,1)} %param.21) | copy-start | bytes 884740
  56.5 14.8 %collective-permute-start.2 = (bf16[18,1,128]{2,1,0:T(2,128)(2,1)S(1)}, bf16[18,1,128]{2,1,0:T(2,128)(2,1)S(1)}, u32[]{:S(2)}, u32[]{:S(2)}) collective-permute-start(bf16[18,1,128]{2,1,0:T(2,128)(2,1)S(1)} %get-tuple-element.37), channel_id=1, source_target_pairs={{0,2},{2,4},{4,6},{1,3},{3,5},{5,7},{8,10},{10,12},{12,14},{9,11},... | collective-permute-start | bytes 13832 | tf_op jit(solution)/shard_map/ppermute | solution.py:16
  69.2 5.0 %collective-permute-start.3 = (bf16[18,1,128]{2,1,0:T(2,128)(2,1)S(1)}, bf16[18,1,128]{2,1,0:T(2,128)(2,1)S(1)}, u32[]{:S(2)}, u32[]{:S(2)}) collective-permute-start(bf16[18,1,128]{2,1,0:T(2,128)(2,1)S(1)} %get-tuple-element.38), channel_id=1, source_target_pairs={{2,0},{4,2},{6,4},{3,1},{5,3},{7,5},{10,8},{12,10},{14,12},{11,9},... | collective-permute-start | bytes 13832 | tf_op jit(solution)/shard_map/ppermute | solution.py:19
Sparse Core Ops, SparseCore 0:
  56.6 31.6 reduce-scatter.3
where the time goes:
time: 97.9 us; the launch traced here: 97 us
  blocking collectives  33.4 us (34%)
  starting transfers between devices  19.9 us (20%)
  waiting for transfers between devices  15.1 us (15%)
  between operations  14.5 us (15%)
  other arithmetic  6.37 us (7%)
  matrix products  4.75 us (5%)
  local copies, waits for them, and re-layouts  3.04 us (3%)
    ppermute x2, starting transfers between devices, padded_2(): lax.ppermute(lax.slice_in_dim(block, block.shape[dim] - width, None, axis...  16.6 us
    unnamed x2, waiting for transfers between devices  12.2 us
    all_gather x1, blocking collectives, per_device(): all_cols = lax.all_gather(col_feat, 'seq', axis=0, tiled=True)  11.3 us
    all_gather x1, blocking collectives, per_device(): key_piece = lax.all_gather(key, 'seq', axis=0, tiled=True)  11.1 us
    all_gather x1, blocking collectives, per_device(): value_piece = lax.all_gather(value, 'seq', axis=0, tiled=True)  11 us
    ppermute x2, starting transfers between devices, padded_2(): lax.ppermute(lax.slice_in_dim(block, 0, width, axis=dim), axis, backward)  3.21 us
    unnamed x26, local copies, waits for them, and re-layouts  2.97 us
    ppermute x2, waiting for transfers between devices, padded_2(): lax.ppermute(lax.slice_in_dim(block, 0, width, axis=dim), axis, backward)  2.87 us
  transfers between devices with their start and end apart: 5, of which 2 were waited for; matrix products, arithmetic and copies ran while one was open for 8% of the time, Pallas kernels for 0%

commit v1 on v0

v1 whole, which is shorter than its diff:
```python
import functools
import math

import jax
import jax.numpy as jnp
import numpy as np
from jax import lax
from jax.experimental import pallas as pl
from jax.experimental.pallas import tpu as pltpu
from jax.sharding import PartitionSpec as P

POOL = 16
EPS = 1e-05
F32 = jnp.float32
BF16 = jnp.bfloat16
MESH = pl.DeviceIdType.MESH


def rope_table(count, size):
    half = size // 2
    freq = 10000.0 ** (-np.arange(half, dtype=np.float64) / half)
    angles = np.arange(count, dtype=np.float64)[:, None] * freq[None, :]
    cosine, sine = np.cos(angles), np.sin(angles)
    return np.concatenate([cosine, cosine, -sine, sine], axis=1).astype(np.float32)


def dot(a, b):
    return jnp.dot(a, b, preferred_element_type=F32)


def kernel(
    n_seq, n_pair,
    embed, attn_gain, w_query, w_key, w_value, w_out, pair_map, w_row, w_col, pair_gain, conv_weight, table,
    block_out, new_pair,
    x_v, gain_v, wqkv, wrc, tab, pm_v, cw, pg_v, nrm, kv, rc, q_v, max_v, sum_v, acc_v, att, wo, res_v,
    hrow, hcol, hcor, colf, colsend, padded, conv_v, out_v, np_v,
    load_s, kv_ss, kv_rs, sib_ss, sib_rs, rc_ss, rc_rs, wo_ss, wo_rs, halo_ss, halo_rs, att_ss, att_rs, out_s,
):
    tokens, width = x_v.shape
    size = kv.shape[2]
    local = q_v.shape[0] // tokens
    rows, cols, chan = pm_v.shape
    bins = rows
    part = res_v.shape[1]
    hw = local * size
    seq, pair = lax.axis_index("seq"), lax.axis_index("pair")
    core = lax.rem(pair, 2)
    sib = pair + 1 - 2 * core

    def seq_of(d):
        return lax.rem(seq + (d + n_seq), n_seq)

    def pair_of(d):
        return lax.rem(pair + (d + n_pair), n_pair)

    loads = {}

    def load(name, src, dst):
        copy = pltpu.make_async_copy(src, dst, load_s.at[len(loads)])
        copy.start()
        loads[name] = copy

    load("x", embed, x_v)
    load("gain", attn_gain, gain_v)
    load("wk", w_key, wqkv.at[:, 0:size])
    load("wv", w_value, wqkv.at[:, size : 2 * size])
    load("tab", table.at[pl.ds(pl.multiple_of(seq * tokens, tokens), tokens)], tab)
    load("wq", w_query, wqkv.at[:, 2 * size : 2 * size + hw])
    load("pm", pair_map, pm_v)
    load("wr", w_row, wrc.at[:, 0:chan])
    load("wc", w_col, wrc.at[:, chan : 2 * chan])
    load("pg", pair_gain, pg_v)
    for i in range(3):
        for j in range(3):
            load(
                ("cw", i, j), conv_weight.at[i, j],
                cw.at[i * chan : (i + 1) * chan, j * chan : (j + 1) * chan],
            )
    mine = pl.ds(pl.multiple_of(pair * part, 128), part)
    load("wo", w_out.at[:, mine], wo.at[pl.ds(pl.multiple_of(pair * hw, 128), hw)])
    load("res", embed.at[:, mine], res_v)

    barrier = pltpu.get_barrier_semaphore()
    count = 0
    for d in range(1, n_seq):
        pl.semaphore_signal(barrier, inc=1, device_id={"seq": seq_of(d)}, device_id_type=MESH)
        count += 1
    for d in range(1, n_pair):
        pl.semaphore_signal(barrier, inc=1, device_id={"pair": pair_of(d)}, device_id_type=MESH)
        count += 1
    for a in (1, -1):
        for b in (1, -1):
            pl.semaphore_signal(
                barrier, inc=1, device_id={"seq": seq_of(a), "pair": pair_of(b)}, device_id_type=MESH
            )
            count += 1

    loads["x"].wait()
    loads["gain"].wait()
    x = x_v[...].astype(F32)
    scale = lax.rsqrt(jnp.mean(x * x, axis=-1, keepdims=True) + EPS)
    nrm[...] = (x * scale * gain_v[...]).astype(BF16)

    pl.semaphore_wait(barrier, count)

    def remote(src, dst, send, recv, **where):
        copy = pltpu.make_async_remote_copy(
            src_ref=src, dst_ref=dst, send_sem=send, recv_sem=recv, device_id=where, device_id_type=MESH
        )
        copy.start()
        return copy

    sent = []
    wo_mine = wo.at[pl.ds(pl.multiple_of(pair * hw, 128), hw)]
    for d in (2, 1, 3) if n_pair == 4 else range(1, n_pair):
        target = pair_of(d)
        sent.append(
            remote(
                w_out.at[:, pl.ds(pl.multiple_of(target * part, 128), part)], wo_mine,
                wo_ss.at[d], wo_rs.at[d], pair=target,
            )
        )

    loads["wk"].wait()
    loads["wv"].wait()
    loads["tab"].wait()
    cc, ss = tab[:, 0:size], tab[:, size : 2 * size]

    def rope(t):
        return t * cc + pltpu.roll(t, size // 2, 1) * ss

    both = dot(nrm[...], wqkv[:, 0 : 2 * size])
    kv[seq, 0:tokens] = rope(both[:, 0:size]).astype(BF16)
    kv[seq, tokens : 2 * tokens] = both[:, size : 2 * size].astype(BF16)
    half = pl.ds(pl.multiple_of(core * tokens, tokens), tokens)

    def offset(i):
        return -((i + 1) // 2) if i % 2 else i // 2

    for i in range(1, n_seq):
        d = -offset(i)
        sent.append(
            remote(
                kv.at[seq, half], kv.at[seq, half], kv_ss.at[i], kv_rs.at[i], seq=seq_of(d)
            )
        )

    loads["pm"].wait()
    for r in range(rows):
        colf[0, r : r + 1] = pm_v[r, cols - 16 : cols].astype(F32)[15:16]
        colf[1, r : r + 1] = pm_v[r, 0:16].astype(F32)[0:1]
    colsend[...] = colf[...].astype(BF16)
    halos = []
    for k, a in enumerate((1, -1)):
        halos.append(
            remote(
                pair_map.at[rows - 1 if a == 1 else 0], hrow.at[k],
                halo_ss.at[k], halo_rs.at[k], seq=seq_of(a),
            )
        )
        halos.append(
            remote(
                colsend.at[k], hcol.at[k], halo_ss.at[2 + k], halo_rs.at[2 + k], pair=pair_of(a)
            )
        )
        for m, b in enumerate((1, -1)):
            slot = 2 * k + m
            halos.append(
                remote(
                    pair_map.at[rows - 1 if a == 1 else 0, pl.ds(cols - 16 if b == 1 else 0, 16)],
                    hcor.at[slot], halo_ss.at[4 + slot], halo_rs.at[4 + slot],
                    seq=seq_of(a), pair=pair_of(b),
                )
            )

    loads["wq"].wait()
    query = dot(nrm[...], wqkv[:, 2 * size : 2 * size + hw])
    for h in range(local):
        q_v[h * tokens : (h + 1) * tokens] = rope(query[:, h * size : (h + 1) * size]).astype(BF16)

    bin_of = lax.broadcasted_iota(jnp.int32, (bins, tokens), 0) * POOL
    at = lax.broadcasted_iota(jnp.int32, (bins, tokens), 1)
    pooler = jnp.where((at >= bin_of) & (at < bin_of + POOL), 1.0 / POOL, 0.0).astype(BF16)
    pooled = dot(pooler, nrm[...]).astype(BF16)
    loads["wr"].wait()
    loads["wc"].wait()
    feats = dot(pooled, wrc[...]).astype(BF16)
    rc[seq, 0:bins] = feats[:, 0:chan]
    rc[seq, bins : 2 * bins] = feats[:, chan : 2 * chan]
    feat_copies = []
    for i in range(1, n_seq):
        feat_copies.append(
            remote(rc.at[seq], rc.at[seq], rc_ss.at[i], rc_rs.at[i], seq=seq_of(-offset(i)))
        )

    factor = math.log2(math.e) / size**0.5
    contract = (((1,), (1,)), ((), ()))

    def attend(b, first):
        scores = lax.dot_general(
            q_v[...], kv[b, 0:tokens], contract, preferred_element_type=F32
        )
        top = jnp.max(scores, axis=-1, keepdims=True)
        if not first:
            old = max_v[...]
            top = jnp.maximum(old, top)
            fix = jnp.exp2((old - top) * factor)
        terms = jnp.exp2((scores - top) * factor)
        total = jnp.sum(terms, axis=-1, keepdims=True)
        mixed = dot(terms.astype(BF16), kv[b, tokens : 2 * tokens])
        max_v[...] = top
        if first:
            sum_v[...] = total
            acc_v[...] = mixed
        else:
            sum_v[...] = sum_v[...] * fix + total
            acc_v[...] = acc_v[...] * fix + mixed

    attend(seq, True)
    forwards = {}

    def receive(i):
        b = seq_of(offset(i))
        pltpu.make_async_remote_copy(
            src_ref=kv.at[b, half], dst_ref=kv.at[b, half], send_sem=kv_ss.at[i], recv_sem=kv_rs.at[i],
            device_id={"seq": b}, device_id_type=MESH,
        ).wait_recv()
        forwards[i] = remote(kv.at[b, half], kv.at[b, half], sib_ss.at[i], sib_rs.at[i], pair=sib)

    for i in range(1, n_seq + 1):
        if i < n_seq:
            receive(i)
        if i > 1:
            forwards[i - 1].wait_recv()
            attend(seq_of(offset(i - 1)), False)

    attended = (acc_v[...] / sum_v[...]).astype(BF16)
    for h in range(local):
        att[pair, :, h * size : (h + 1) * size] = attended[h * tokens : (h + 1) * tokens]

    chips = n_pair // 2
    across = []
    for d in range(1, chips):
        across.append(
            remote(
                att.at[pair], att.at[pair], att_ss.at[d], att_rs.at[d],
                pair=lax.rem(pair + 2 * d, n_pair),
            )
        )
    near = remote(att.at[pair], att.at[pair], att_ss.at[0], att_rs.at[0], pair=sib)

    for copy in halos + feat_copies:
        copy.wait_recv()
    for name in loads:
        if name == "pg" or name[0] == "cw":
            loads[name].wait()
    pg = pg_v[...]

    def normal(u):
        return u * lax.rsqrt(jnp.mean(u * u, axis=-1, keepdims=True) + EPS) * pg

    own = rc[seq].astype(F32)
    row_main = own[0:bins]
    row_low = rc[seq_of(-1)].astype(F32)[bins - 1 : bins]
    row_high = rc[seq_of(1)].astype(F32)[0:1]
    per = cols // bins
    col_main = jnp.concatenate(
        [rc[pair * per + j, bins : 2 * bins].astype(F32) for j in range(per)], axis=0
    )
    col_low = rc[lax.rem(pair * per + (n_seq - 1), n_seq)].astype(F32)[2 * bins - 1 : 2 * bins]
    col_high = rc[lax.rem(pair * per + per, n_seq)].astype(F32)[bins : bins + 1]
    has = [
        jnp.where(seq > 0, 1.0, 0.0), jnp.where(seq < n_seq - 1, 1.0, 0.0),
        jnp.where(pair > 0, 1.0, 0.0), jnp.where(pair < n_pair - 1, 1.0, 0.0),
    ]
    padded[...] = jnp.zeros_like(padded)
    updated = pm_v[...].astype(F32) + row_main[:, None, :] * col_main[None, :, :]
    padded[1 : rows + 1, 8 : 8 + cols] = normal(updated)
    padded[0, 8 : 8 + cols] = normal(hrow[0].astype(F32) + row_low * col_main) * has[0]
    padded[rows + 1, 8 : 8 + cols] = normal(hrow[1].astype(F32) + row_high * col_main) * has[1]
    low = normal(hcol[0].astype(F32) + row_main * col_low) * has[2]
    high = normal(hcol[1].astype(F32) + row_main * col_high) * has[3]
    for r in range(rows):
        padded[1 + r, 7:8] = low[r : r + 1]
        padded[1 + r, 8 + cols : 9 + cols] = high[r : r + 1]
    for k, rf in enumerate((row_low, row_high)):
        for m, cf in enumerate((col_low, col_high)):
            corner = hcor[2 * k + m].astype(F32)
            corner = corner[15:16] if m == 0 else corner[0:1]
            place = 7 if m == 0 else 8 + cols
            padded[0 if k == 0 else rows + 1, place : place + 1] = (
                normal(corner + rf * cf) * (has[k] * has[2 + m])
            )
    wide = padded.shape[1]
    window = jnp.concatenate(
        [padded[i : i + rows].reshape(rows * wide, chan).astype(BF16) for i in range(3)], axis=1
    )
    conv_v[...] = dot(window, cw[...]).reshape(rows, wide, 3 * chan)
    total = updated
    for j in range(3):
        total = total + conv_v[:, 7 + j : 7 + j + cols, j * chan : (j + 1) * chan]
    np_v[...] = total.astype(BF16)
    pair_done = pltpu.make_async_copy(np_v, new_pair, out_s.at[0])
    pair_done.start()

    passed = []
    for d in range(1, chips):
        across[d - 1].wait_recv()
        other = lax.rem(pair + (n_pair - 2 * d), n_pair)
        passed.append(
            remote(att.at[other], att.at[other], att_ss.at[chips + d], att_rs.at[chips + d], pair=sib)
        )
    loads["wo"].wait()
    loads["res"].wait()
    for copy in sent[: n_pair - 1]:
        copy.wait_recv()

    def term(p):
        return dot(att[p], wo[pl.ds(pl.multiple_of(p * hw, 128), hw)])

    result = res_v[...].astype(F32) + term(pair)
    for d in range(1, chips):
        result = result + term(lax.rem(pair + (n_pair - 2 * d), n_pair))
    near.wait_recv()
    result = result + term(sib)
    for d in range(1, chips):
        passed[d - 1].wait_recv()
        result = result + term(lax.rem(sib + (n_pair - 2 * d), n_pair))
    out_v[...] = result.astype(BF16)
    out_done = pltpu.make_async_copy(out_v, block_out, out_s.at[1])
    out_done.start()
    for copy in sent + halos + feat_copies + list(forwards.values()) + across + [near] + passed:
        copy.wait_send()
    pair_done.wait()
    out_done.wait()


def per_device(
    embed, attn_gain, w_query, w_key, w_value, w_out, pair_map, w_row, w_col, pair_gain, conv_weight
):
    n_seq, n_pair = lax.axis_size("seq"), lax.axis_size("pair")
    tokens, width = embed.shape
    size = w_key.shape[1]
    hw = w_query.shape[1]
    local = hw // size
    rows, cols, chan = pair_map.shape
    part = width // n_pair
    bins = tokens // POOL
    wide = cols + 16
    table = jnp.asarray(rope_table(n_seq * tokens, size))
    dma = pltpu.SemaphoreType.DMA
    vmem = pltpu.VMEM
    return pl.pallas_call(
        functools.partial(kernel, n_seq, n_pair),
        out_shape=[
            jax.ShapeDtypeStruct((tokens, part), BF16),
            jax.ShapeDtypeStruct(pair_map.shape, BF16),
        ],
        in_specs=[pl.BlockSpec(memory_space=pl.ANY)] * 12,
        out_specs=[pl.BlockSpec(memory_space=pl.ANY)] * 2,
        scratch_shapes=[
            vmem((tokens, width), BF16),
            vmem((1, width), F32),
            vmem((width, 2 * size + hw), BF16),
            vmem((width, 2 * chan), BF16),
            vmem((tokens, 2 * size), F32),
            vmem((rows, cols, chan), BF16),
            vmem((3 * chan, 3 * chan), BF16),
            vmem((1, chan), F32),
            vmem((tokens, width), BF16),
            vmem((n_seq, 2 * tokens, size), BF16),
            vmem((n_seq, 2 * bins, chan), BF16),
            vmem((local * tokens, size), BF16),
            vmem((local * tokens, 1), F32),
            vmem((local * tokens, 1), F32),
            vmem((local * tokens, size), F32),
            vmem((n_pair, tokens, hw), BF16),
            vmem((n_pair * hw, part), BF16),
            vmem((tokens, part), BF16),
            vmem((2, cols, chan), BF16),
            vmem((2, rows, chan), BF16),
            vmem((4, 16, chan), BF16),
            vmem((2, rows, chan), F32),
            vmem((2, rows, chan), BF16),
            vmem((rows + 2, wide, chan), F32),
            vmem((rows, wide, 3 * chan), F32),
            vmem((tokens, part), BF16),
            vmem((rows, cols, chan), BF16),
            dma((21,)),
            dma((n_seq,)),
            dma((n_seq,)),
            dma((n_seq,)),
            dma((n_seq,)),
            dma((n_seq,)),
            dma((n_seq,)),
            dma((n_pair,)),
            dma((n_pair,)),
            dma((8,)),
            dma((8,)),
            dma((n_pair,)),
            dma((n_pair,)),
            dma((2,)),
        ],
        compiler_params=pltpu.CompilerParams(
            collective_id=0, has_side_effects=True, vmem_limit_bytes=56 * 1024 * 1024
        ),
    )(
        embed, attn_gain.reshape(1, width), w_query, w_key, w_value, w_out, pair_map, w_row, w_col,
        pair_gain.reshape(1, chan), conv_weight, table,
    )


def solution(mesh):
    placed = (
        P(("dp", "seq"), None),
        P(),
        P(None, "pair"),
        P(),
        P(),
        P("pair", None),
        P(("dp", "seq"), "pair", None),
        P(),
        P(),
        P(),
        P(),
    )
    return jax.shard_map(
        per_device,
        mesh=mesh,
        in_specs=placed,
        out_specs=(P(("dp", "seq"), "pair"), P(("dp", "seq"), "pair", None)),
        check_vma=False,
    )
```

time: 97.9 us -> 28.9 us (0.30)
  blocking collectives: 33.4 us -> 0 us
  Pallas kernels: 0 us -> 24.4 us
  starting transfers between devices: 19.9 us -> 0 us
  waiting for transfers between devices: 15.1 us -> 0 us
  between operations: 14.5 us -> 0.65 us
  other arithmetic: 6.37 us -> 0 us
  matrix products: 4.75 us -> 0 us
    all_gather x3 -> x0, blocking collectives: 33.4 us -> none  [the longest x1 11.3 us: per_device(): all_cols = lax.all_gather(col_feat, 'seq', axis=0, tiled=True)]
    pallas_call x0 -> x1, Pallas kernels: none -> 24.4 us  [per_device(): pl.pallas_call(functools.partial(kernel, n_seq, n_pair), out_shape=[jax.S...]
    ppermute x4 -> x0, starting transfers between devices: 19.9 us -> none  [the longest x2 16.6 us: padded_2(): lax.ppermute(lax.slice_in_dim(block, block.shape[dim] - width, None, axis...]
    unnamed x2 -> x0, waiting for transfers between devices: 12.2 us -> none
    dot_general x17 -> x0, matrix products: 4.75 us -> none  [the longest x9 1.31 us: per_device(): jnp.dot(window.reshape(row_count * column_count, channel_count), conv_wei...]
    reduce_sum x4 -> x0, other arithmetic: 3.8 us -> none  [the longest x1 1.67 us: per_device(): jnp.mean(normed.astype(jnp.float32).reshape(tokens // POOL, POOL, model_w...]
    ppermute x4 -> x0, waiting for transfers between devices: 2.87 us -> none  [the longest x2 2.87 us: padded_2(): lax.ppermute(lax.slice_in_dim(block, 0, width, axis=dim), axis, backward)]
    convert_element_type x5 -> x0, other arithmetic: 1.5 us -> none  [the longest x1 0.74 us: per_device(): block_out = (residual.astype(jnp.float32) + summed).astype(jnp.bfloat16)]
  transfers between devices with their start and end apart: 5 -> 0, of which waited for: 2 -> 0; matrix products, arithmetic and copies ran while one was open for 8% -> 0% of each run, Pallas kernels for 0% -> 0%
where the time goes in v1:
time: 28.9 us; the launch traced here: 28.7 us
  Pallas kernels  24.4 us (84%)
  local copies, waits for them, and re-layouts  3.58 us (12%)
  between operations  0.65 us (2%)
    pallas_call x1, Pallas kernels, per_device(): pl.pallas_call(functools.partial(kernel, n_seq, n_pair), out_shape=[jax.S...  24.4 us
    unnamed x4, local copies, waits for them, and re-layouts  2.29 us
    reshape x1, local copies, waits for them, and re-layouts, per_device(): attn_gain.reshape(1, width)  1.3 us

profile of v1, /device:TPU:1, one launch (start us, length us, event | category | flops | bytes accessed | tf_op | source)
XLA Modules:
  0.0 28.7 jit_solution(11270645803174509909)
XLA Ops:
  0.6 1.3 %reshape.10.attn_gain = f32[1,1536]{1,0:T(1,128)} reshape(f32[1536]{0:T(1024)} %param.13) | data formatting | bytes 12288 | tf_op jit(solution)/shard_map/reshape | solution.py:408
  1.9 24.4 %shard_map.131 = (bf16[256,384]{1,0:T(8,128)(2,1)}, bf16[16,16,128]{2,1,0:T(8,128)(2,1)}) custom-call(bf16[256,1536]{1,0:T(8,128)(2,1)} %embed.1, f32[1,1536]{1,0:T(1,128)} %reshape.10.attn_gain, bf16[1536,256]{1,0:T(8,128)(2,1)} %w_query.1, bf16[1536,128]{1,0:T(8,128)(2,1)} %w_key.1, bf16[1536,128]{1,0:T(8,128)(2,1)} %w_value.1, bf16[256,1536]{1,0:T(8,128)(2,1)} %w_out.1, ...), custom_call_target="tpu_custom_call" | custom-call | tf_op jit(solution)/shard_map/pallas_call | solution.py:353
  26.4 0.0 copy-start
  26.4 1.7 %copy.16 = bf16[256,384]{1,0:T(8,128)(2,1)} copy(bf16[256,384]{1,0:T(8,128)(2,1)} %get-tuple-element.4) | data formatting | bytes 393216
  28.0 0.0 copy-done
  28.0 0.6 %copy.17 = bf16[16,16,128]{2,1,0:T(8,128)(2,1)} copy(bf16[16,16,128]{2,1,0:T(8,128)(2,1)S(1)} %copy-done) | data formatting | bytes 131072
Async XLA Ops:
  26.4 1.7 %copy-start = (bf16[16,16,128]{2,1,0:T(8,128)(2,1)S(1)}, bf16[16,16,128]{2,1,0:T(8,128)(2,1)}, u32[]{:S(2)}) copy-start(bf16[16,16,128]{2,1,0:T(8,128)(2,1)} %get-tuple-element.5) | copy-start | bytes 196612

commit v2 on v1

--- a/solution.py
+++ b/solution.py
@@ -99,7 +99,7 @@
     loads["gain"].wait()
     x = x_v[...].astype(F32)
     scale = lax.rsqrt(jnp.mean(x * x, axis=-1, keepdims=True) + EPS)
-    nrm[...] = (x * scale * gain_v[...]).astype(BF16)
+    nrm[...] = (x * scale * gain_v[...][None, :]).astype(BF16)
 
     pl.semaphore_wait(barrier, count)
 
@@ -335,6 +335,11 @@
     out_done.wait()
 
 
+def hand_on(a, b, c, d):
+    c[...] = a[...]
+    d[...] = b[...]
+
+
 def per_device(
     embed, attn_gain, w_query, w_key, w_value, w_out, pair_map, w_row, w_col, pair_gain, conv_weight
 ):
@@ -350,7 +355,7 @@
     table = jnp.asarray(rope_table(n_seq * tokens, size))
     dma = pltpu.SemaphoreType.DMA
     vmem = pltpu.VMEM
-    return pl.pallas_call(
+    outs = pl.pallas_call(
         functools.partial(kernel, n_seq, n_pair),
         out_shape=[
             jax.ShapeDtypeStruct((tokens, part), BF16),
@@ -360,7 +365,7 @@
         out_specs=[pl.BlockSpec(memory_space=pl.ANY)] * 2,
         scratch_shapes=[
             vmem((tokens, width), BF16),
-            vmem((1, width), F32),
+            vmem((width,), F32),
             vmem((width, 2 * size + hw), BF16),
             vmem((width, 2 * chan), BF16),
             vmem((tokens, 2 * size), F32),
@@ -405,9 +410,15 @@
             collective_id=0, has_side_effects=True, vmem_limit_bytes=56 * 1024 * 1024
         ),
     )(
-        embed, attn_gain.reshape(1, width), w_query, w_key, w_value, w_out, pair_map, w_row, w_col,
+        embed, attn_gain, w_query, w_key, w_value, w_out, pair_map, w_row, w_col,
         pair_gain.reshape(1, chan), conv_weight, table,
     )
+    return pl.pallas_call(
+        hand_on,
+        out_shape=[jax.ShapeDtypeStruct(o.shape, o.dtype) for o in outs],
+        in_specs=[pl.BlockSpec(memory_space=pltpu.VMEM)] * 2,
+        out_specs=[pl.BlockSpec(memory_space=pltpu.VMEM)] * 2,
+    )(*outs)
 
 
 def solution(mesh):

time: 28.9 us -> 26.9 us (0.931)
  local copies, waits for them, and re-layouts: 3.58 us -> 0 us
  Pallas kernels: 24.4 us -> 26.1 us
    unnamed x4 -> x0, local copies, waits for them, and re-layouts: 2.29 us -> none
    pallas_call x0 -> x1, Pallas kernels: none -> 1.65 us  [per_device(): pl.pallas_call(hand_on, out_shape=[jax.ShapeDtypeStruct(o.shape, o.dtype)...]
    reshape x1 -> x0, local copies, waits for them, and re-layouts: 1.3 us -> none  [per_device(): attn_gain.reshape(1, width)]
where the time goes in v2:
time: 26.9 us; the launch traced here: 26.8 us
  Pallas kernels  26.1 us (97%)
  between operations  0.64 us (2%)
    pallas_call x1, Pallas kernels, per_device(): pl.pallas_call(functools.partial(kernel, n_seq, n_pair), out_shape=[jax.S...  24.5 us
    pallas_call x1, Pallas kernels, per_device(): pl.pallas_call(hand_on, out_shape=[jax.ShapeDtypeStruct(o.shape, o.dtype)...  1.65 us

profile of v2, /device:TPU:1, one launch (start us, length us, event | category | flops | bytes accessed | tf_op | source)
XLA Modules:
  0.0 26.8 jit_solution(3177533844836108061)
XLA Ops:
  0.6 24.5 %shard_map.131 = (bf16[256,384]{1,0:T(8,128)(2,1)}, bf16[16,16,128]{2,1,0:T(8,128)(2,1)}) custom-call(bf16[256,1536]{1,0:T(8,128)(2,1)} %embed.1, f32[1536]{0:T(1024)} %attn_gain.1, bf16[1536,256]{1,0:T(8,128)(2,1)} %w_query.1, bf16[1536,128]{1,0:T(8,128)(2,1)} %w_key.1, bf16[1536,128]{1,0:T(8,128)(2,1)} %w_value.1, bf16[256,1536]{1,0:T(8,128)(2,1)} %w_out.1, ...), custom_call_target="tpu_custom_call" | custom-call | tf_op jit(solution)/shard_map/pallas_call | solution.py:358
  25.1 1.6 %shard_map.132 = (bf16[256,384]{1,0:T(8,128)(2,1)}, bf16[16,16,128]{2,1,0:T(8,128)(2,1)}) custom-call(bf16[256,384]{1,0:T(8,128)(2,1)} %get-tuple-element.4.a, bf16[16,16,128]{2,1,0:T(8,128)(2,1)} %get-tuple-element.5.b), custom_call_target="tpu_custom_call" | custom-call | tf_op jit(solution)/shard_map/pallas_call | solution.py:416

commit v3 on v2

--- a/solution.py
+++ b/solution.py
@@ -67,18 +67,6 @@
     load("tab", table.at[pl.ds(pl.multiple_of(seq * tokens, tokens), tokens)], tab)
     load("wq", w_query, wqkv.at[:, 2 * size : 2 * size + hw])
     load("pm", pair_map, pm_v)
-    load("wr", w_row, wrc.at[:, 0:chan])
-    load("wc", w_col, wrc.at[:, chan : 2 * chan])
-    load("pg", pair_gain, pg_v)
-    for i in range(3):
-        for j in range(3):
-            load(
-                ("cw", i, j), conv_weight.at[i, j],
-                cw.at[i * chan : (i + 1) * chan, j * chan : (j + 1) * chan],
-            )
-    mine = pl.ds(pl.multiple_of(pair * part, 128), part)
-    load("wo", w_out.at[:, mine], wo.at[pl.ds(pl.multiple_of(pair * hw, 128), hw)])
-    load("res", embed.at[:, mine], res_v)
 
     barrier = pltpu.get_barrier_semaphore()
     count = 0
@@ -172,6 +160,19 @@
                     seq=seq_of(a), pair=pair_of(b),
                 )
             )
+
+    load("wr", w_row, wrc.at[:, 0:chan])
+    load("wc", w_col, wrc.at[:, chan : 2 * chan])
+    load("pg", pair_gain, pg_v)
+    for i in range(3):
+        for j in range(3):
+            load(
+                ("cw", i, j), conv_weight.at[i, j],
+                cw.at[i * chan : (i + 1) * chan, j * chan : (j + 1) * chan],
+            )
+    mine = pl.ds(pl.multiple_of(pair * part, 128), part)
+    load("wo", w_out.at[:, mine], wo.at[pl.ds(pl.multiple_of(pair * hw, 128), hw)])
+    load("res", embed.at[:, mine], res_v)
 
     loads["wq"].wait()
     query = dot(nrm[...], wqkv[:, 2 * size : 2 * size + hw])
@@ -241,12 +242,14 @@
     chips = n_pair // 2
     across = []
     for d in range(1, chips):
-        across.append(
-            remote(
-                att.at[pair], att.at[pair], att_ss.at[d], att_rs.at[d],
-                pair=lax.rem(pair + 2 * d, n_pair),
-            )
-        )
+        for piece in range(2):
+            held = att.at[pair, piece * tokens // 2 : (piece + 1) * tokens // 2]
+            across.append(
+                remote(
+                    held, held, att_ss.at[2 * d + piece], att_rs.at[2 * d + piece],
+                    pair=lax.rem(pair + 2 * d, n_pair),
+                )
+            )
     near = remote(att.at[pair], att.at[pair], att_ss.at[0], att_rs.at[0], pair=sib)
 
     for copy in halos + feat_copies:
@@ -305,11 +308,12 @@
 
     passed = []
     for d in range(1, chips):
-        across[d - 1].wait_recv()
         other = lax.rem(pair + (n_pair - 2 * d), n_pair)
-        passed.append(
-            remote(att.at[other], att.at[other], att_ss.at[chips + d], att_rs.at[chips + d], pair=sib)
-        )
+        for piece in range(2):
+            across[2 * d - 2 + piece].wait_recv()
+            held = att.at[other, piece * tokens // 2 : (piece + 1) * tokens // 2]
+            slot = 2 * (chips + d) + piece
+            passed.append(remote(held, held, att_ss.at[slot], att_rs.at[slot], pair=sib))
     loads["wo"].wait()
     loads["res"].wait()
     for copy in sent[: n_pair - 1]:
@@ -324,7 +328,8 @@
     near.wait_recv()
     result = result + term(sib)
     for d in range(1, chips):
-        passed[d - 1].wait_recv()
+        passed[2 * d - 2].wait_recv()
+        passed[2 * d - 1].wait_recv()
         result = result + term(lax.rem(sib + (n_pair - 2 * d), n_pair))
     out_v[...] = result.astype(BF16)
     out_done = pltpu.make_async_copy(out_v, block_out, out_s.at[1])
@@ -402,8 +407,8 @@
             dma((n_pair,)),
             dma((8,)),
             dma((8,)),
-            dma((n_pair,)),
-            dma((n_pair,)),
+            dma((2 * n_pair,)),
+            dma((2 * n_pair,)),
             dma((2,)),
         ],
         compiler_params=pltpu.CompilerParams(

time: 26.9 us -> 26.9 us (level)
  no operation moved by 1% of the time
where the time goes in v3:
time: 26.9 us; the launch traced here: 26.7 us
  Pallas kernels  26.1 us (97%)
  between operations  0.64 us (2%)
    pallas_call x1, Pallas kernels, per_device(): pl.pallas_call(functools.partial(kernel, n_seq, n_pair), out_shape=[jax.S...  24.4 us
    pallas_call x1, Pallas kernels, per_device(): pl.pallas_call(hand_on, out_shape=[jax.ShapeDtypeStruct(o.shape, o.dtype)...  1.65 us

profile of v3, /device:TPU:1, one launch (start us, length us, event | category | flops | bytes accessed | tf_op | source)
XLA Modules:
  0.0 26.7 jit_solution(13788867081003159074)
XLA Ops:
  0.6 24.4 %shard_map.131 = (bf16[256,384]{1,0:T(8,128)(2,1)}, bf16[16,16,128]{2,1,0:T(8,128)(2,1)}) custom-call(bf16[256,1536]{1,0:T(8,128)(2,1)} %embed.1, f32[1536]{0:T(1024)} %attn_gain.1, bf16[1536,256]{1,0:T(8,128)(2,1)} %w_query.1, bf16[1536,128]{1,0:T(8,128)(2,1)} %w_key.1, bf16[1536,128]{1,0:T(8,128)(2,1)} %w_value.1, bf16[256,1536]{1,0:T(8,128)(2,1)} %w_out.1, ...), custom_call_target="tpu_custom_call" | custom-call | tf_op jit(solution)/shard_map/pallas_call | solution.py:363
  25.1 1.6 %shard_map.132 = (bf16[256,384]{1,0:T(8,128)(2,1)}, bf16[16,16,128]{2,1,0:T(8,128)(2,1)}) custom-call(bf16[256,384]{1,0:T(8,128)(2,1)} %get-tuple-element.4.a, bf16[16,16,128]{2,1,0:T(8,128)(2,1)} %get-tuple-element.5.b), custom_call_target="tpu_custom_call" | custom-call | tf_op jit(solution)/shard_map/pallas_call | solution.py:421
